TPU v7x, 32 devices: a whole 2x2x4 slice. The times are simulated.
32 devices in a mesh: gy: 8 (over z, core), gx: 4 (over y, x).
Axes of the slice: x: 2, y: 2, z: 4, core: 2. Of those that a mesh axis runs over, the one named last changes fastest.
Arguments:
- incoming_activations: bfloat16 [192, 64, 1024], P(None, 'gy', 'gx'), may hold values from -75 to 75
- upstream_adjoint: bfloat16 [192, 64, 1024], P(None, 'gy', 'gx'), may hold values from -30 to 30
- standardize_factor: float32 [192], replicated, may hold values from 0.1 to 1.9
- standardize_offset: float32 [192], replicated, may hold values from -3 to 3
- triple_mapping_matrix: bfloat16 [576, 192], replicated, may hold values from -0.4375 to 0.4375
- spatial_filter_taps: float32 [3, 3, 576], replicated, may hold values from -2 to 2
- sharpness_factor: float32 [4], replicated, may hold values from 1 to 8
- output_mapping_matrix: bfloat16 [192, 192], replicated, may hold values from -0.4375 to 0.4375
Outputs:
- incoming_activation_adjoint: bfloat16 [192, 64, 1024], P(None, 'gy', 'gx')
- triple_mapping_adjoint: float32 [576, 192], replicated
- spatial_filter_adjoint: float32 [3, 3, 576], replicated
- output_mapping_adjoint: float32 [192, 192], replicated
- sharpness_factor_adjoint: float32 [4], replicated
- standardize_factor_adjoint: float32 [192], replicated
- standardize_offset_adjoint: float32 [192], replicated
All inputs are finite; a program needn't handle non-finite values.
Results may differ from a plain program's by a relative error of at most 0.0063.
Values may be sent and summed in bfloat16 or wider, within the bound.
A program may use at most 128 MiB of HBM per device.

v0:
```python
import jax
import jax.numpy as jnp
from jax import lax
from jax.sharding import PartitionSpec as P

ATTENDER_TOTAL = 4
HD = 48


def extended(block, sides, width):
    for axis, dim in sides:
        count = lax.axis_size(axis)
        forward = [(i, i + 1) for i in range(count - 1)]
        backward = [(target, source) for source, target in forward]
        low = lax.ppermute(
            lax.slice_in_dim(block, block.shape[dim] - width, None, axis=dim), axis, forward
        )
        high = lax.ppermute(lax.slice_in_dim(block, 0, width, axis=dim), axis, backward)
        block = jnp.concatenate([low, block, high], axis=dim)
    return block


def conv_padded(padded, tap_weights, tile_rows, tile_cols):
    summed = jnp.zeros((padded.shape[0], tile_rows, tile_cols), jnp.float32)
    for row_off in range(3):
        for col_off in range(3):
            window = padded[:, row_off : row_off + tile_rows, col_off : col_off + tile_cols].astype(
                jnp.float32
            )
            summed = summed + tap_weights[row_off, col_off][:, None, None] * window
    return summed


def body(
    incoming_activations,
    upstream_adjoint,
    standardize_factor,
    standardize_offset,
    triple_mapping_matrix,
    spatial_filter_taps,
    sharpness_factor,
    output_mapping_matrix,
):
    f32 = jnp.float32
    half_precision_type = jnp.bfloat16
    channels, tile_rows, tile_cols = incoming_activations.shape
    cell_count = tile_rows * tile_cols
    qkv_width = triple_mapping_matrix.shape[0]
    pixel_total = float(cell_count * lax.axis_size("gy") * lax.axis_size("gx"))
    x_flat = incoming_activations.astype(f32).reshape(channels, cell_count)
    average = jnp.mean(x_flat, axis=0, keepdims=True)
    centred = x_flat - average
    inv_std = 1.0 / jnp.sqrt(jnp.mean(centred * centred, axis=0, keepdims=True) + 1e-05)
    x_hat = centred * inv_std
    normed = (x_hat * standardize_factor[:, None] + standardize_offset[:, None]).astype(
        half_precision_type
    )
    projected = jnp.dot(triple_mapping_matrix, normed, preferred_element_type=f32).astype(
        half_precision_type
    )
    padded = extended(projected.reshape(qkv_width, tile_rows, tile_cols), (("gy", 1), ("gx", 2)), 1)
    conv_out = (
        conv_padded(padded, spatial_filter_taps, tile_rows, tile_cols)
        .astype(half_precision_type)
        .reshape(3, ATTENDER_TOTAL, HD, cell_count)
    )
    queries, key_rows, value_rows = (conv_out[0], conv_out[1], conv_out[2])
    q_f32 = queries.astype(f32)
    k_f32 = key_rows.astype(f32)
    squares_q = jnp.sum(q_f32 * q_f32, axis=2)
    squares_k = jnp.sum(k_f32 * k_f32, axis=2)
    similarity_matrix = jnp.einsum("hin,hjn->hij", queries, key_rows, preferred_element_type=f32)
    grad_flat = upstream_adjoint.reshape(channels, cell_count)
    grad_attended = jnp.einsum(
        "cd,cn->dn", output_mapping_matrix, grad_flat, preferred_element_type=f32
    ).astype(half_precision_type)
    grad_attended = grad_attended.reshape(ATTENDER_TOTAL, HD, cell_count)
    attend_local = jnp.einsum("hin,hjn->hij", grad_attended, value_rows, preferred_element_type=f32)
    squares_q, squares_k, similarity_matrix = lax.psum(
        (squares_q, squares_k, similarity_matrix), ("gy", "gx")
    )
    unit_probe_vectors = jnp.sqrt(squares_q + 1e-06)
    unit_lookup_vectors = jnp.sqrt(squares_k + 1e-06)
    affinity_matrix = (
        sharpness_factor[:, None, None]
        * similarity_matrix
        / (unit_probe_vectors[:, :, None] * unit_lookup_vectors[:, None, :])
    )
    expo = jnp.exp(affinity_matrix)
    attend = expo / jnp.sum(expo, axis=2, keepdims=True)
    attend_low = attend.astype(half_precision_type)
    attended = jnp.einsum(
        "hij,hjn->hin", attend_low, value_rows, preferred_element_type=f32
    ).astype(half_precision_type)
    attended = attended.reshape(channels, cell_count)
    proj_term = (
        jnp.einsum("cn,dn->cd", grad_flat, attended, preferred_element_type=f32) / pixel_total
    )
    proj_total = lax.psum(proj_term, ("gy", "gx"))
    grad_attend = lax.psum(attend_local, ("gy", "gx"))
    grad_values = jnp.einsum("hij,hin->hjn", attend_low, grad_attended, preferred_element_type=f32)
    affinity_matrix_adjoint = attend * (
        grad_attend - jnp.sum(attend * grad_attend, axis=2, keepdims=True)
    )
    mixed_content_vectors = affinity_matrix_adjoint * affinity_matrix
    sharpness_factor_adjoint = (
        jnp.sum(mixed_content_vectors, axis=(1, 2)) / sharpness_factor / pixel_total
    )
    row_terms = jnp.sum(mixed_content_vectors, axis=2)
    col_terms = jnp.sum(mixed_content_vectors, axis=1)
    plane_mixing_matrix = (
        sharpness_factor[:, None, None]
        * affinity_matrix_adjoint
        / (unit_probe_vectors[:, :, None] * unit_lookup_vectors[:, None, :])
    ).astype(half_precision_type)
    grad_queries = jnp.einsum(
        "hij,hjn->hin", plane_mixing_matrix, key_rows, preferred_element_type=f32
    )
    grad_queries = grad_queries - (row_terms / (squares_q + 1e-06))[:, :, None] * q_f32
    grad_keys = jnp.einsum("hij,hin->hjn", plane_mixing_matrix, queries, preferred_element_type=f32)
    grad_keys = grad_keys - (col_terms / (squares_k + 1e-06))[:, :, None] * k_f32
    grad_conv = (
        jnp.stack([grad_queries, grad_keys, grad_values])
        .astype(half_precision_type)
        .reshape(qkv_width, tile_rows, tile_cols)
    )
    grad_pad = extended(grad_conv, (("gy", 1), ("gx", 2)), 1)
    grad_projected = conv_padded(
        grad_pad, spatial_filter_taps[::-1, ::-1], tile_rows, tile_cols
    ).astype(half_precision_type)
    grad_projected = grad_projected.reshape(qkv_width, cell_count)
    grad_conv_f32 = grad_conv.astype(f32)
    tap_rows = []
    for row_off in range(3):
        tap_line = []
        for col_off in range(3):
            window = padded[:, row_off : row_off + tile_rows, col_off : col_off + tile_cols].astype(
                f32
            )
            tap_line.append(jnp.sum(grad_conv_f32 * window, axis=(1, 2)))
        tap_rows.append(jnp.stack(tap_line))
    depth_term = jnp.stack(tap_rows) / pixel_total
    depth_total = lax.psum(depth_term, ("gy", "gx"))
    qkv_term = (
        jnp.einsum("rn,cn->rc", grad_projected, normed, preferred_element_type=f32) / pixel_total
    )
    grad_normed = jnp.einsum(
        "rc,rn->cn", triple_mapping_matrix, grad_projected, preferred_element_type=f32
    )
    gain_term = jnp.sum(grad_normed * x_hat, axis=1) / pixel_total
    bias_term = jnp.sum(grad_normed, axis=1) / pixel_total
    qkv_total, gain_total, bias_total = lax.psum((qkv_term, gain_term, bias_term), ("gy", "gx"))
    grad_hat = grad_normed * standardize_factor[:, None]
    centre_term = jnp.mean(grad_hat, axis=0, keepdims=True)
    slope_term = jnp.mean(grad_hat * x_hat, axis=0, keepdims=True)
    incoming_activation_adjoint = grad_flat.astype(f32) + inv_std * (
        grad_hat - centre_term - x_hat * slope_term
    )
    incoming_activation_adjoint = incoming_activation_adjoint.astype(half_precision_type).reshape(
        channels, tile_rows, tile_cols
    )
    return (
        incoming_activation_adjoint,
        qkv_total,
        depth_total,
        proj_total,
        sharpness_factor_adjoint,
        gain_total,
        bias_total,
    )


def solution(mesh):
    in_specs = (P(None, "gy", "gx"), P(None, "gy", "gx"), P(), P(), P(), P(), P(), P())
    out_specs = (P(None, "gy", "gx"), P(), P(), P(), P(), P(), P())
    return jax.shard_map(body, mesh=mesh, in_specs=in_specs, out_specs=out_specs, check_vma=False)
```

profile of v0, /device:TPU:0, one launch (start us, length us, event | category | flops | bytes accessed | tf_op | source)
XLA Modules:
  0.0 462.4 jit_solution(10784306177397411633)
XLA Ops:
  18.2 3.8 collective-permute-start
  22.6 3.4 copy.47
  26.0 4.0 copy.42
  37.2 4.8 %pad_maximum_fusion = bf16[576,10,256]{0,1,2:T(8,128)(2,1)S(1)} fusion(bf16[576,1,256]{0,1,2:T(2,128)(2,1)S(1)} %copy.43, bf16[576,8,256]{0,1,2:T(8,128)(2,1)S(1)} %copy-done.11, bf16[576,1,256]{0,1,2:T(2,128)(2,1)} %copy.41), kind=kLoop, calls=%fused_computation.41 | loop fusion | flops 8847360 | bytes 5898240 | tf_op jit(solution)/shard_map/concatenate | solution.py:19
  42.6 5.4 %collective-permute-start.2 = (bf16[576,10,1]{0,1,2:T(8,128)(2,1)S(1)}, bf16[576,10,1]{0,1,2:T(8,128)(2,1)}, u32[]{:S(2)}, u32[]{:S(2)}) collective-permute-start(bf16[576,10,1]{0,1,2:T(8,128)(2,1)S(1)} %get-tuple-element.73), channel_id=1, source_target_pairs={{0,1},{1,2},{2,3},{4,5},{5,6},{6,7},{8,9},{9,10},{10,11},{12,13},{... | collective-permute-start | bytes 34568 | tf_op jit(solution)/shard_map/ppermute | solution.py:15
  49.5 2.9 constant_dynamic-update-slice_fusion
  58.3 11.7 %fusion.9 = bf16[576,8,256]{0,2,1:T(8,128)(2,1)S(1)} fusion(bf16[576,8,256]{0,2,1:T(8,128)(2,1)} %copy.47, bf16[576,1,256]{0,2,1:T(8,128)(2,1)} %copy.52, bf16[576,1,256]{0,2,1:T(8,128)(2,1)} %copy.46, f32[576]{0:T(1024)} %get-tuple-element.56, f32[576]{0:T(1024)} %get-tuple-element.57, f32[576]{0:T(1024)} %get-tuple-element.50, f32[576]{0:T(1024)} %get-tuple-element.51, ...), kind=kLoop, calls=%fused_computation.26 | loop fusion | flops 49545216 | bytes 15367680 | tf_op jit(solution)/shard_map/convert_element_type | solution.py:64
  96.8 123.8 %all-reduce.6.cloned.1.call-done = (f32[4,48]{1,0:T(4,128)}, f32[4,48]{1,0:T(4,128)}, f32[4,48,48]{2,1,0:T(8,128)}, f32[4,48,48]{2,1,0:T(8,128)}) async-done(((f32[4,48]{1,0:T(4,128)}, f32[4,48]{1,0:T(4,128)}, f32[4,48,48]{2,1,0:T(8,128)}, f32[4,48,48]{2,1,0:T(8,128)}), (f32[4,48]{1,0:T(4,128)}, f32[4,48]{1,0:T(4,128)}, f32[4,48,48]{2,1,0:T(8,128)}, f32[4,48,48]{2,1,0:T(8,128)})) %all-reduce.6.cloned.1.call-update) | async-done | bytes 75280 | tf_op jit(solution)/shard_map/psum | solution.py:79
  223.1 2.6 convolution_bitcast_fusion
  231.2 3.9 fusion.29
  235.1 3.4 fusion.30
  245.7 4.8 %copy.66 = bf16[576,8,256]{0,2,1:T(8,128)(2,1)} copy(bf16[576,8,256]{2,1,0:T(8,128)(2,1)} %bitcast.72) | data formatting | bytes 4718592 | tf_op jit(solution)/shard_map/convert_element_type | solution.py:124
  251.9 3.6 fusion.24
  260.5 3.7 collective-permute-start.4
  264.2 10.7 %fusion.16 = (f32[576]{0:T(1024)S(1)}, f32[576]{0:T(1024)S(1)}, f32[576]{0:T(1024)S(1)}, f32[576]{0:T(1024)S(1)}, f32[576]{0:T(1024)S(1)}, /*index=5*/f32[576]{0:T(1024)S(1)}, f32[576]{0:T(1024)S(1)}, f32[576]{0:T(1024)S(1)}) fusion(bf16[576,8,256]{0,2,1:T(8,128)(2,1)} %copy.66, bf16[576,10,256]{0,2,1:T(8,128)(2,1)S(1)} %get-tuple-element.70, ...), kind=kLoop, calls=%fused_computation.33 | loop fusion | flops 47181312 | bytes 15365376 | tf_op jit(solution)/shard_map/reduce_sum | solution.py:140
  275.1 5.5 %copy.61 = bf16[576,8,256]{0,1,2:T(8,128)(2,1)} copy(bf16[576,8,256]{2,1,0:T(8,128)(2,1)} %bitcast.73) | data formatting | bytes 4718592 | tf_op jit(solution)/shard_map/convert_element_type | solution.py:124
  284.6 5.1 %pad_maximum_fusion.1 = bf16[576,10,256]{0,1,2:T(8,128)(2,1)S(1)} fusion(bf16[576,1,256]{0,1,2:T(2,128)(2,1)S(1)} %copy.62, bf16[576,8,256]{0,1,2:T(8,128)(2,1)} %copy.61, bf16[576,1,256]{0,1,2:T(2,128)(2,1)S(1)} %copy.60), kind=kLoop, calls=%fused_computation.42 | loop fusion | flops 8847360 | bytes 5898240 | tf_op jit(solution)/shard_map/concatenate | solution.py:19
  291.5 5.4 %collective-permute-start.6 = (bf16[576,10,1]{0,1,2:T(8,128)(2,1)}, bf16[576,10,1]{0,1,2:T(8,128)(2,1)}, u32[]{:S(2)}, u32[]{:S(2)}) collective-permute-start(bf16[576,10,1]{0,1,2:T(8,128)(2,1)} %get-tuple-element.72), channel_id=1, source_target_pairs={{0,1},{1,2},{2,3},{4,5},{5,6},{6,7},{8,9},{9,10},{10,11},{12,13},{... | collective-permute-start | bytes 34568 | tf_op jit(solution)/shard_map/ppermute | solution.py:15
  296.9 3.9 constant_dynamic-update-slice_fusion.1
  305.3 11.4 %fusion.15 = bf16[576,8,256]{0,2,1:T(8,128)(2,1)S(1)} fusion(bf16[576,8,256]{0,2,1:T(8,128)(2,1)S(1)} %copy-done.6, bf16[576,10,256]{0,2,1:T(8,128)(2,1)} %get-tuple-element.68, bf16[576,10,1]{0,2,1:T(2,128)(2,1)S(1)} %copy.63, bf16[576,10,257]{0,2,1:T(8,128)(2,1)} %copy_dynamic-update-slice_fusion, bf16[576,1,256]{0,2,1:T(8,128)(2,1)S(1)} %copy.71, ...), kind=kLoop, calls=%fused_computation.32 | loop fusion | flops 49545216 | bytes 15367680 | tf_op jit(solution)/shard_map/convert_element_type | solution.py:130
  319.8 3.0 fusion.31
  322.8 2.6 add_convert_fusion.1
  327.8 41.4 %all-reduce = (f32[3,3,576]{2,1,0:T(4,128)}, f32[192]{0:T(256)}, f32[192]{0:T(256)}) all-reduce(f32[3,3,576]{2,1,0:T(4,128)S(1)} %maximum_multiply_fusion, f32[192]{0:T(256)S(1)} %broadcast_multiply_fusion.4, f32[192]{0:T(256)S(1)} %broadcast_multiply_fusion.3), channel_id=1, replica_groups=mesh['gy'=8,'gx'=4] {'gy','gx'}, use_global_device_ids=true, to_apply=%region_24.0 | all-reduce | flops 5568 | bytes 44544 | tf_op jit(solution)/shard_map/psum | solution.py:143
  369.2 82.8 %all-reduce.8.cloned.1.call-done = (f32[576,192]{0,1:T(8,128)}, f32[192,192]{0,1:T(8,128)}) async-done(((f32[576,192]{0,1:T(8,128)}, f32[192,192]{0,1:T(8,128)}), (f32[576,192]{0,1:T(8,128)}, f32[192,192]{0,1:T(8,128)})) %all-reduce.8.cloned.1.call-update) | async-done | bytes 589840 | tf_op jit(solution)/shard_map/psum | solution.py:152
  (163 shorter events, 94.2 us)
Async XLA Ops:
  7.2 213.4 %all-reduce.6.cloned.1.call-start = ((), (), s32[]{:S(2)}) async-start(), calls=%async_computation | async-start | bytes 401408 | tf_op jit(solution)/shard_map/psum | solution.py:79
  14.6 7.4 %copy-start.26 = (f32[3,3,576]{2,1,0:T(4,128)S(1)}, f32[3,3,576]{2,1,0:T(4,128)}, u32[]{:S(2)}) copy-start(f32[3,3,576]{2,1,0:T(4,128)} %param.13) | copy-start | bytes 62212
  16.2 17.5 %collective-permute-start.1 = (bf16[576,1,256]{2,0,1:T(8,128)(2,1)S(1)}, bf16[576,1,256]{2,0,1:T(8,128)(2,1)}, u32[]{:S(2)}, u32[]{:S(2)}) collective-permute-start(bf16[576,1,256]{2,0,1:T(8,128)(2,1)S(1)} %copy.81), channel_id=1, source_target_pairs={{4,0},{8,4},{12,8},{16,12},{20,16},{24,20},{28,24},{5,1},{9,5},{13... | collective-permute-start | bytes 884744 | tf_op jit(solution)/shard_map/ppermute | solution.py:18
  18.2 16.9 %collective-permute-start = (bf16[576,1,256]{2,0,1:T(8,128)(2,1)}, bf16[576,1,256]{2,0,1:T(8,128)(2,1)}, u32[]{:S(2)}, u32[]{:S(2)}) collective-permute-start(bf16[576,1,256]{2,0,1:T(8,128)(2,1)} %copy.80), channel_id=1, source_target_pairs={{0,4},{4,8},{8,12},{12,16},{16,20},{20,24},{24,28},{1,5},{5,9},{9,... | collective-permute-start | bytes 884744 | tf_op jit(solution)/shard_map/ppermute | solution.py:15
  22.6 35.6 %copy-start.23 = (f32[576]{0:T(1024)}, f32[576]{0:T(1024)S(1)}, u32[]{:S(2)}) copy-start(f32[576]{0:T(1024)S(1)} %get-tuple-element.49) | copy-start | bytes 6916
  42.6 13.6 %collective-permute-start.2 = (bf16[576,10,1]{0,1,2:T(8,128)(2,1)S(1)}, bf16[576,10,1]{0,1,2:T(8,128)(2,1)}, u32[]{:S(2)}, u32[]{:S(2)}) collective-permute-start(bf16[576,10,1]{0,1,2:T(8,128)(2,1)S(1)} %get-tuple-element.73), channel_id=1, source_target_pairs={{0,1},{1,2},{2,3},{4,5},{5,6},{6,7},{8,9},{9,10},{10,11},{12,13},{... | collective-permute-start | bytes 34568 | tf_op jit(solution)/shard_map/ppermute | solution.py:15
  48.0 8.9 %collective-permute-start.3 = (bf16[576,10,1]{0,1,2:T(8,128)(2,1)}, bf16[576,10,1]{0,1,2:T(8,128)(2,1)}, u32[]{:S(2)}, u32[]{:S(2)}) collective-permute-start(bf16[576,10,1]{0,1,2:T(8,128)(2,1)} %get-tuple-element.74), channel_id=1, source_target_pairs={{1,0},{2,1},{3,2},{5,4},{6,5},{7,6},{9,8},{10,9},{11,10},{13,12},{... | collective-permute-start | bytes 34568 | tf_op jit(solution)/shard_map/ppermute | solution.py:18
  84.7 9.5 %copy-start.28 = (f32[192]{0:T(256)S(1)}, f32[192]{0:T(256)}, u32[]{:S(2)}) copy-start(f32[192]{0:T(256)} %param.10) | copy-start | bytes 2308
  94.0 358.0 %all-reduce.8.cloned.1.call-start = ((), (), s32[]{:S(2)}) async-start(), calls=%async_computation.1 | async-start | bytes 1376256 | tf_op jit(solution)/shard_map/psum | solution.py:152
  220.6 7.6 %copy-start.15 = (f32[4,48,48]{2,1,0:T(8,128)S(1)}, f32[4,48,48]{2,1,0:T(8,128)}, u32[]{:S(2)}) copy-start(f32[4,48,48]{2,1,0:T(8,128)} %get-tuple-element.63) | copy-start | bytes 110596
  220.6 7.7 %copy-start.34 = (f32[4,48,48]{2,1,0:T(8,128)S(1)}, f32[4,48,48]{2,1,0:T(8,128)}, u32[]{:S(2)}) copy-start(f32[4,48,48]{2,1,0:T(8,128)} %get-tuple-element.64) | copy-start | bytes 110596
  220.6 10.1 %copy-start.30 = (f32[4,48]{1,0:T(4,128)S(1)}, f32[4,48]{1,0:T(4,128)}, u32[]{:S(2)}) copy-start(f32[4,48]{1,0:T(4,128)} %get-tuple-element.61) | copy-start | bytes 2308
  220.6 10.1 %copy-start.31 = (f32[4,48]{1,0:T(4,128)S(1)}, f32[4,48]{1,0:T(4,128)}, u32[]{:S(2)}) copy-start(f32[4,48]{1,0:T(4,128)} %get-tuple-element.62) | copy-start | bytes 2308
  222.0 8.6 %copy-start.24 = (f32[4,48]{1,0:T(4,128)}, f32[4,48]{1,0:T(4,128)S(1)}, u32[]{:S(2)}) copy-start(f32[4,48]{1,0:T(4,128)S(1)} %add_sqrt_fusion.1) | copy-start | bytes 2308
  223.1 7.5 %copy-start.25 = (f32[4,48]{1,0:T(4,128)}, f32[4,48]{1,0:T(4,128)S(1)}, u32[]{:S(2)}) copy-start(f32[4,48]{1,0:T(4,128)S(1)} %exponential_reduce_fusion) | copy-start | bytes 2308
  250.5 13.7 %copy-start.1 = (bf16[576,10,257]{0,2,1:T(8,128)(2,1)S(1)}, bf16[576,10,257]{0,2,1:T(8,128)(2,1)}, u32[]{:S(2)}) copy-start(bf16[576,10,257]{0,2,1:T(8,128)(2,1)} %copy_dynamic-update-slice_fusion.1) | copy-start | bytes 8881924
  250.5 13.7 %copy-start.5 = (bf16[576,8,256]{0,2,1:T(8,128)(2,1)S(1)}, bf16[576,8,256]{0,2,1:T(8,128)(2,1)}, u32[]{:S(2)}) copy-start(bf16[576,8,256]{0,2,1:T(8,128)(2,1)} %copy.47) | copy-start | bytes 7077892
  250.5 13.7 %copy-start.14 = (bf16[576,1,256]{0,2,1:T(8,128)(2,1)S(1)}, bf16[576,1,256]{0,2,1:T(8,128)(2,1)}, u32[]{:S(2)}) copy-start(bf16[576,1,256]{0,2,1:T(8,128)(2,1)} %copy.46) | copy-start | bytes 884740
  259.2 22.5 %collective-permute-start.5 = (bf16[576,1,256]{2,0,1:T(8,128)(2,1)}, bf16[576,1,256]{2,0,1:T(8,128)(2,1)}, u32[]{:S(2)}, u32[]{:S(2)}) collective-permute-start(bf16[576,1,256]{2,0,1:T(8,128)(2,1)} %copy.83), channel_id=1, source_target_pairs={{4,0},{8,4},{12,8},{16,12},{20,16},{24,20},{28,24},{5,1},{9,5},{13... | collective-permute-start | bytes 884744 | tf_op jit(solution)/shard_map/ppermute | solution.py:18
  260.5 22.7 %collective-permute-start.4 = (bf16[576,1,256]{2,0,1:T(8,128)(2,1)}, bf16[576,1,256]{2,0,1:T(8,128)(2,1)}, u32[]{:S(2)}, u32[]{:S(2)}) collective-permute-start(bf16[576,1,256]{2,0,1:T(8,128)(2,1)} %copy.82), channel_id=1, source_target_pairs={{0,4},{4,8},{8,12},{12,16},{16,20},{20,24},{24,28},{1,5},{5,9},{9,... | collective-permute-start | bytes 884744 | tf_op jit(solution)/shard_map/ppermute | solution.py:15
  290.2 13.7 %collective-permute-start.7 = (bf16[576,10,1]{0,1,2:T(8,128)(2,1)}, bf16[576,10,1]{0,1,2:T(8,128)(2,1)}, u32[]{:S(2)}, u32[]{:S(2)}) collective-permute-start(bf16[576,10,1]{0,1,2:T(8,128)(2,1)} %get-tuple-element.71), channel_id=1, source_target_pairs={{1,0},{2,1},{3,2},{5,4},{6,5},{7,6},{9,8},{10,9},{11,10},{13,12},{... | collective-permute-start | bytes 34568 | tf_op jit(solution)/shard_map/ppermute | solution.py:18
  291.5 13.8 %copy-start.6 = (bf16[576,8,256]{0,2,1:T(8,128)(2,1)S(1)}, bf16[576,8,256]{0,2,1:T(8,128)(2,1)}, u32[]{:S(2)}) copy-start(bf16[576,8,256]{0,2,1:T(8,128)(2,1)} %copy.66) | copy-start | bytes 7077892
  291.5 11.6 %collective-permute-start.6 = (bf16[576,10,1]{0,1,2:T(8,128)(2,1)}, bf16[576,10,1]{0,1,2:T(8,128)(2,1)}, u32[]{:S(2)}, u32[]{:S(2)}) collective-permute-start(bf16[576,10,1]{0,1,2:T(8,128)(2,1)} %get-tuple-element.72), channel_id=1, source_target_pairs={{0,1},{1,2},{2,3},{4,5},{5,6},{6,7},{8,9},{9,10},{10,11},{12,13},{... | collective-permute-start | bytes 34568 | tf_op jit(solution)/shard_map/ppermute | solution.py:15
  305.3 12.9 %copy-start.16 = (bf16[192,8,256]{2,1,0:T(8,128)(2,1)S(1)}, bf16[192,8,256]{2,1,0:T(8,128)(2,1)}, u32[]{:S(2)}) copy-start(bf16[192,8,256]{2,1,0:T(8,128)(2,1)} %add_convert_fusion) | copy-start | bytes 2359300
  (21 other events, 70.1 us)
Sparse Core Ops, SparseCore 0:
  94.1 126.4 all-reduce.5
  322.9 129.0 all-reduce.7
where the time goes:
time: 465 us; the launch traced here: 462 us
  waiting for transfers between devices  207 us (45%)
  local copies, waits for them, and re-layouts  84.7 us (18%)
  other arithmetic  66.2 us (14%)
  blocking collectives  41.4 us (9%)
  matrix products  24.9 us (5%)
  starting transfers between devices  24 us (5%)
  between operations  14.6 us (3%)
    psum x1, waiting for transfers between devices, body(): lax.psum((squares_q, squares_k, similarity_matrix), ('gy', 'gx'))  124 us
    psum x1, waiting for transfers between devices, body(): lax.psum((qkv_term, gain_term, bias_term), ('gy', 'gx'))  82.8 us
    psum x1, blocking collectives, body(): depth_total = lax.psum(depth_term, ('gy', 'gx'))  41.4 us
    unnamed x85, local copies, waits for them, and re-layouts  28.2 us
    ppermute x4, starting transfers between devices, extended(): lax.ppermute(lax.slice_in_dim(block, block.shape[dim] - width, None, axis...  18.4 us
    reduce_sum x2, other arithmetic, body(): tap_line.append(jnp.sum(grad_conv_f32 * window, axis=(1, 2)))  14.3 us
    convert_element_type x1, other arithmetic, body(): conv_out = conv_padded(padded, spatial_filter_taps, tile_rows, tile_cols)...  11.7 us
    convert_element_type x1, other arithmetic, body(): grad_projected = conv_padded(grad_pad, spatial_filter_taps[::-1, ::-1], t...  11.4 us
  transfers between devices with their start and end apart: 10, of which 2 were waited for; matrix products, arithmetic and copies ran while one was open for 12% of the time, Pallas kernels for 0%

commit v1 on v0

v1 whole, which is shorter than its diff:
```python
import functools

import jax
import jax.numpy as jnp
import numpy as np
from jax import lax
from jax.experimental import pallas as pl
from jax.experimental.pallas import tpu as pltpu
from jax.sharding import PartitionSpec as P

ATTENDER_TOTAL = 4
HD = 48
F32 = jnp.float32
BF16 = jnp.bfloat16
MESH = pl.DeviceIdType.MESH
VMEM = pl.BlockSpec(memory_space=pltpu.VMEM)
SMEM = pl.BlockSpec(memory_space=pltpu.SMEM)
NT = (((1,), (1,)), ((), ()))
TN = (((0,), (0,)), ((), ()))
LIMIT = 56 * 1024 * 1024
SIDE = 16


def dot(a, b, dims=(((1,), (0,)), ((), ()))):
    return lax.dot_general(a, b, dims, preferred_element_type=F32)


def dot_full(a, b, dims=(((1,), (0,)), ((), ()))):
    return lax.dot_general(
        a, b, dims, preferred_element_type=F32, precision=lax.Precision.HIGHEST
    )


def front_kernel(rows, cols, x_ref, gain_ref, bias_ref, w_ref, sel_ref,
                 p_ref, normed_ref, stat_ref, edge_ref):
    channels = x_ref.shape[0]
    gain = gain_ref[...]
    bias = bias_ref[...]
    edge = jnp.zeros((2 * SIDE, channels), F32)
    normed_ref[pl.ds(channels, normed_ref.shape[0] - channels), :] = jnp.zeros(
        (normed_ref.shape[0] - channels, rows * cols), BF16
    )
    stat_ref[...] = jnp.zeros_like(stat_ref)
    for y in range(rows):
        at = pl.ds(y * cols, cols)
        x = x_ref[:, at].astype(F32)
        mean = jnp.sum(x, axis=0, keepdims=True) / channels
        centred = x - mean
        var = jnp.sum(centred * centred, axis=0, keepdims=True) / channels
        inv = 1.0 / jnp.sqrt(var + 1e-05)
        stat_ref[pl.ds(0, 1), at] = mean
        stat_ref[pl.ds(1, 1), at] = inv
        normed = ((centred * inv) * gain + bias).astype(BF16)
        normed_ref[pl.ds(0, channels), at] = normed
        p_ref[:, at] = dot(w_ref[...], normed).astype(BF16)
        edge = edge + dot(sel_ref[:, at], normed, NT)
    edge_ref[...] = dot(edge.astype(BF16), w_ref[...], NT).astype(BF16)


def halo_kernel(cols, p_ref, edge_ref, top_ref, bot_ref, side_ref, send, recv):
    gy, gx = lax.axis_index("gy"), lax.axis_index("gx")
    ny, nx = lax.axis_size("gy"), lax.axis_size("gx")
    tail = p_ref.shape[1] - cols
    moves = []
    for dy in (-1, 0, 1):
        for dx in (-1, 0, 1):
            if dy or dx:
                moves.append((dy, dx))

    def there(dy, dx):
        ty, tx = gy + dy, gx + dx
        return (ty >= 0) & (ty < ny) & (tx >= 0) & (tx < nx), (ty, tx)

    barrier = pltpu.get_barrier_semaphore()
    for dy, dx in moves:
        ok, target = there(dy, dx)

        @pl.when(ok)
        def _(target=target):
            pl.semaphore_signal(barrier, inc=1, device_id=target, device_id_type=MESH)

    down = 1 + (gy > 0).astype(jnp.int32) + (gy < ny - 1).astype(jnp.int32)
    across = 1 + (gx > 0).astype(jnp.int32) + (gx < nx - 1).astype(jnp.int32)
    pl.semaphore_wait(barrier, down * across - 1)

    def copy(k, dy, dx, target):
        if dx == 0:
            src = p_ref.at[:, pl.ds(0 if dy < 0 else tail, cols)]
            dst = bot_ref if dy < 0 else top_ref
        else:
            src = edge_ref.at[pl.ds(0 if dx < 0 else SIDE, SIDE)]
            dst = side_ref.at[1 if dx < 0 else 0, 1 - dy]
        return pltpu.make_async_remote_copy(
            src_ref=src, dst_ref=dst, send_sem=send.at[k], recv_sem=recv.at[k],
            device_id=target, device_id_type=MESH,
        )

    for k, (dy, dx) in enumerate(moves):
        ok, target = there(dy, dx)

        @pl.when(ok)
        def _(k=k, dy=dy, dx=dx, target=target):
            copy(k, dy, dx, target).start()

    for k, (dy, dx) in enumerate(moves):
        ok, target = there(-dy, -dx)
        back, other = there(dy, dx)

        @pl.when(ok)
        def _(k=k, dy=dy, dx=dx, target=target):
            copy(k, dy, dx, target).wait_recv()

        @pl.when(jnp.logical_not(ok))
        def _(k=k, dy=dy, dx=dx):
            if dx == 0:
                ref = bot_ref if dy < 0 else top_ref
                ref[...] = jnp.zeros_like(ref)
            else:
                side_ref[1 if dx < 0 else 0, 1 - dy] = jnp.zeros(side_ref.shape[2:], BF16)

        @pl.when(back)
        def _(k=k, dy=dy, dx=dx, other=other):
            copy(k, dy, dx, other).wait_send()


def halo(p, edge, cols, collective_id):
    width = p.shape[0]
    return pl.pallas_call(
        functools.partial(halo_kernel, cols),
        out_shape=(
            jax.ShapeDtypeStruct((width, cols), BF16),
            jax.ShapeDtypeStruct((width, cols), BF16),
            jax.ShapeDtypeStruct((2, 3, SIDE, width), BF16),
        ),
        in_specs=[VMEM] * 2,
        out_specs=(VMEM,) * 3,
        scratch_shapes=[pltpu.SemaphoreType.DMA((8,)), pltpu.SemaphoreType.DMA((8,))],
        compiler_params=pltpu.CompilerParams(
            collective_id=collective_id, has_side_effects=True, vmem_limit_bytes=LIMIT
        ),
    )(p, edge)


def shift_rows(rows, cols, p_ref, top_ref, bot_ref, side_ref, shift_ref, spread_ref, moved):
    width = p_ref.shape[0]
    for y in range(rows + 2):
        at = pl.ds(y * cols, cols)
        if y == 0:
            row = top_ref[...]
        elif y == rows + 1:
            row = bot_ref[...]
        else:
            row = p_ref[:, pl.ds((y - 1) * cols, cols)]
        for side in range(2):
            edge = side_ref[side].reshape(3 * SIDE, width)
            fill = dot(edge, spread_ref[side, :, at], TN)
            moved[side, :, at] = (dot(row, shift_ref[side]) + fill).astype(BF16)


def conv_kernel(rows, cols, p_ref, top_ref, bot_ref, side_ref, shift_ref, spread_ref, taps_ref,
                g_ref, conv_ref, part_ref, moved, squares):
    width = p_ref.shape[0]
    channels = width // 3
    part_rows = part_ref.shape[0]
    shift_rows(rows, cols, p_ref, top_ref, bot_ref, side_ref, shift_ref, spread_ref, moved)

    def chunk(i, carry):
        rs = pl.ds(pl.multiple_of(i * 16, 16), 16)
        taps = [jnp.broadcast_to(taps_ref[rs, pl.ds(k, 1)], (16, 128)) for k in range(9)]
        total = jnp.zeros((16, 128), F32)
        for half in range(cols // 128):
            got = {}
            for y in range(rows + 2):
                at = pl.ds(y * cols + half * 128, 128)
                if y == 0:
                    mid = top_ref[rs, pl.ds(half * 128, 128)]
                elif y == rows + 1:
                    mid = bot_ref[rs, pl.ds(half * 128, 128)]
                else:
                    mid = p_ref[rs, pl.ds((y - 1) * cols + half * 128, 128)]
                got[y] = (moved[0, rs, at].astype(F32), mid.astype(F32), moved[1, rs, at].astype(F32))
                if y >= 2:
                    out = jnp.zeros((16, 128), F32)
                    for a in range(3):
                        for b in range(3):
                            out = out + taps[3 * a + b] * got[y - 2 + a][b]
                    out = out.astype(BF16)
                    conv_ref[rs, pl.ds((y - 2) * cols + half * 128, 128)] = out
                    out = out.astype(F32)
                    total = total + out * out
        squares[rs, :] = jnp.broadcast_to(jnp.sum(total, axis=1, keepdims=True), (16, 128))
        return carry

    lax.fori_loop(0, width // 16, chunk, 0)
    queries = conv_ref[pl.ds(0, channels), :]
    keys = conv_ref[pl.ds(channels, channels), :]
    values = conv_ref[pl.ds(2 * channels, channels), :]
    gram = dot(queries, keys, NT)
    mixed = dot(g_ref[...], values, NT)
    lane = lax.broadcasted_iota(jnp.int32, (HD, channels), 1) // HD
    compact = jnp.zeros((HD, channels), F32)
    for h in range(channels // HD):
        compact = compact + jnp.where(lane == h, gram[h * HD:(h + 1) * HD, :], 0.0)
    pad = jnp.zeros((channels, 256 - channels), F32)
    lanes = lax.broadcasted_iota(jnp.int32, (channels, 128), 1)
    high = jnp.concatenate([mixed[:, 128:], pad], axis=1)
    high = jnp.where(lanes == 64, squares[pl.ds(0, channels), :], high)
    high = jnp.where(lanes == 65, squares[pl.ds(channels, channels), :], high)
    span = channels + HD
    part_ref[pl.ds(0, channels), :] = mixed[:, :128]
    part_ref[pl.ds(channels, HD), :] = compact[:, :128]
    part_ref[pl.ds(span, channels), :] = high
    part_ref[pl.ds(span + channels, HD), :] = jnp.concatenate(
        [compact[:, 128:], pad[:HD]], axis=1
    )
    part_ref[pl.ds(2 * span, part_rows - 2 * span), :] = jnp.zeros((part_rows - 2 * span, 128), F32)


def sum_kernel(in_ref, out_ref, got_x, held, got_y, send, recv):
    gy, gx = lax.axis_index("gy"), lax.axis_index("gx")
    ny, nx = lax.axis_size("gy"), lax.axis_size("gx")
    barrier = pltpu.get_barrier_semaphore()
    for d in range(1, nx):
        pl.semaphore_signal(barrier, inc=1, device_id=(gy, lax.rem(gx + d, nx)), device_id_type=MESH)
    for d in range(1, ny):
        pl.semaphore_signal(barrier, inc=1, device_id=(lax.rem(gy + d, ny), gx), device_id_type=MESH)
    pl.semaphore_wait(barrier, nx + ny - 2)

    slot = 0

    def exchange(copies):
        nonlocal slot
        made = []
        for src, dst, target in copies:
            made.append(pltpu.make_async_remote_copy(
                src_ref=src, dst_ref=dst, send_sem=send.at[slot], recv_sem=recv.at[slot],
                device_id=target, device_id_type=MESH,
            ))
            slot += 1
            made[-1].start()
        for copy in made:
            copy.wait()

    exchange([
        (in_ref.at[lax.rem(gx + d, nx)], got_x.at[d - 1], (gy, lax.rem(gx + d, nx)))
        for d in range(1, nx)
    ])
    total = in_ref[gx]
    for d in range(1, nx):
        total = total + got_x[d - 1]
    held[...] = total
    exchange([
        (held.at[lax.rem(gy + d, ny)], got_y.at[d - 1], (lax.rem(gy + d, ny), gx))
        for d in range(1, ny)
    ])
    total = held[gy]
    for d in range(1, ny):
        total = total + got_y[d - 1]
    out_ref[gx, gy] = total
    exchange([
        (out_ref.at[gx, gy], out_ref.at[gx, gy], (lax.rem(gy + d, ny), gx)) for d in range(1, ny)
    ])
    exchange([
        (out_ref.at[gx], out_ref.at[gx], (gy, lax.rem(gx + d, nx))) for d in range(1, nx)
    ])


def sum_over_devices(part, collective_id):
    ny, nx = lax.axis_size("gy"), lax.axis_size("gx")
    piece = part.shape[0] // (nx * ny)
    count = 2 * (nx + ny - 2)
    shape = (nx, ny, piece, 128)
    out = pl.pallas_call(
        sum_kernel,
        out_shape=jax.ShapeDtypeStruct(shape, F32),
        in_specs=[VMEM],
        out_specs=VMEM,
        scratch_shapes=[
            pltpu.VMEM((nx - 1, ny, piece, 128), F32),
            pltpu.VMEM((ny, piece, 128), F32),
            pltpu.VMEM((ny - 1, piece, 128), F32),
            pltpu.SemaphoreType.DMA((count,)),
            pltpu.SemaphoreType.DMA((count,)),
        ],
        compiler_params=pltpu.CompilerParams(
            collective_id=collective_id, has_side_effects=True, vmem_limit_bytes=LIMIT
        ),
    )(part.reshape(shape))
    return out.reshape(part.shape)


def padded_rows(count):
    unit = 8 * lax.axis_size("gy") * lax.axis_size("gx")
    return -(-count // unit) * unit


def attend_kernel(texels, tot_ref, sharp_ref, wo_ref, conv_ref, g_ref, sel_ref,
                  grad_ref, edge_ref, omap_ref, sharp_adj_ref):
    channels = wo_ref.shape[0]
    span = channels + HD
    low, high = tot_ref[pl.ds(0, channels), :], tot_ref[pl.ds(span, channels), :]
    mixed = jnp.concatenate([low, high[:, :channels - 128]], axis=1)
    sq, sk = high[:, 64:65], high[:, 65:66]
    compact = jnp.concatenate(
        [tot_ref[pl.ds(channels, HD), :], tot_ref[pl.ds(span + channels, HD), :][:, :channels - 128]],
        axis=1,
    )
    heads = channels // HD
    gram = jnp.concatenate([compact] * heads, axis=0)
    rows = lax.broadcasted_iota(jnp.int32, (channels, channels), 0)
    lanes = lax.broadcasted_iota(jnp.int32, (channels, channels), 1)
    same = (rows // HD) == (lanes // HD)
    eye = rows == lanes
    head = lax.broadcasted_iota(jnp.int32, (channels, 1), 0) // HD
    sharp = jnp.zeros((channels, 1), F32)
    for h in range(heads):
        sharp = jnp.where(head == h, sharp_ref[h], sharp)

    def to_row(col):
        return jnp.sum(jnp.where(eye, col, 0.0), axis=0, keepdims=True)

    def to_col(row):
        return jnp.sum(jnp.where(eye, row, 0.0), axis=1, keepdims=True)

    norms = jnp.sqrt(sq + 1e-06) * jnp.sqrt(to_row(sk) + 1e-06)
    logits = jnp.where(same, sharp * gram / norms, 0.0)
    expo = jnp.where(same, jnp.exp(logits), 0.0)
    attend = expo / jnp.sum(expo, axis=1, keepdims=True)
    attend_low = attend.astype(BF16)
    omap_ref[...] = dot_full(mixed, attend_low.astype(F32), NT) / texels
    grad_attend = dot_full(wo_ref[...].astype(F32), mixed, TN)
    grad_logits = attend * (grad_attend - jnp.sum(attend * grad_attend, axis=1, keepdims=True))
    product = grad_logits * logits
    row_terms = jnp.sum(product, axis=1, keepdims=True)
    col_terms = to_col(jnp.sum(product, axis=0, keepdims=True))
    for h in range(heads):
        sharp_adj_ref[h] = jnp.sum(jnp.where(head == h, row_terms, 0.0)) / sharp_ref[h] / texels
    coupling = (sharp * grad_logits / norms).astype(BF16)
    row_scale = row_terms / (sq + 1e-06)
    col_scale = col_terms / (sk + 1e-06)
    cells = conv_ref.shape[1]
    step = 256
    edges = [jnp.zeros((2 * SIDE, channels), F32) for _ in range(3)]
    for n in range(cells // step):
        at = pl.ds(n * step, step)
        queries = conv_ref[pl.ds(0, channels), at]
        keys = conv_ref[pl.ds(channels, channels), at]
        grad_attended = dot(wo_ref[...], g_ref[:, at], TN).astype(BF16)
        grads = (
            dot(coupling, keys) - row_scale * queries.astype(F32),
            dot(coupling, queries, TN) - col_scale * keys.astype(F32),
            dot(attend_low, grad_attended, TN),
        )
        for i, grad in enumerate(grads):
            grad = grad.astype(BF16)
            grad_ref[pl.ds(i * channels, channels), at] = grad
            edges[i] = edges[i] + dot(sel_ref[:, at], grad, NT)
    edge_ref[...] = jnp.concatenate(edges, axis=1).astype(BF16)


def back_kernel(rows, cols, texels, grad_ref, top_ref, bot_ref, side_ref, shift_ref, spread_ref,
                taps_ref, p_ref, normed_ref, w_ref, x_ref, stat_ref, gain_ref, g_ref,
                out_ref, part_ref, moved, gp_ref, sums):
    width = grad_ref.shape[0]
    channels = width // 3
    part_rows = part_ref.shape[0]
    shift_rows(rows, cols, grad_ref, top_ref, bot_ref, side_ref, shift_ref, spread_ref, moved)

    def chunk(i, carry):
        rs = pl.ds(pl.multiple_of(i * 16, 16), 16)
        taps = [jnp.broadcast_to(taps_ref[rs, pl.ds(k, 1)], (16, 128)) for k in range(9)]
        tap_sums = [jnp.zeros((16, 128), F32) for _ in range(9)]
        for half in range(cols // 128):
            got = {}
            for y in range(rows + 2):
                at = pl.ds(y * cols + half * 128, 128)
                if y == 0:
                    mid = top_ref[rs, pl.ds(half * 128, 128)]
                elif y == rows + 1:
                    mid = bot_ref[rs, pl.ds(half * 128, 128)]
                else:
                    mid = grad_ref[rs, pl.ds((y - 1) * cols + half * 128, 128)]
                got[y] = (moved[0, rs, at].astype(F32), mid.astype(F32), moved[1, rs, at].astype(F32))
                if y >= 2:
                    here = pl.ds((y - 2) * cols + half * 128, 128)
                    field = p_ref[rs, here].astype(F32)
                    out = jnp.zeros((16, 128), F32)
                    for a in range(3):
                        for b in range(3):
                            k = 3 * (2 - a) + (2 - b)
                            out = out + taps[k] * got[y - 2 + a][b]
                            tap_sums[k] = tap_sums[k] + field * got[y - 2 + a][b]
                    gp_ref[rs, here] = out.astype(BF16)
        lane = lax.broadcasted_iota(jnp.int32, (16, 128), 1)
        packed = jnp.zeros((16, 128), F32)
        for k in range(9):
            packed = jnp.where(lane == 64 + k, jnp.sum(tap_sums[k], axis=1, keepdims=True), packed)
        sums[rs, :] = packed
        return carry

    lax.fori_loop(0, width // 16, chunk, 0)
    gain = gain_ref[...]
    gain_sum = jnp.zeros((channels, cols), F32)
    bias_sum = jnp.zeros((channels, cols), F32)
    for y in range(rows):
        at = pl.ds(y * cols, cols)
        grad_normed = dot(w_ref[...], gp_ref[:, at], TN)
        mean, inv = stat_ref[pl.ds(0, 1), at], stat_ref[pl.ds(1, 1), at]
        x_hat = (x_ref[:, at].astype(F32) - mean) * inv
        gain_sum = gain_sum + grad_normed * x_hat
        bias_sum = bias_sum + grad_normed
        grad_hat = grad_normed * gain
        centre = jnp.sum(grad_hat, axis=0, keepdims=True) / channels
        slope = jnp.sum(grad_hat * x_hat, axis=0, keepdims=True) / channels
        out = g_ref[:, at].astype(F32) + inv * (grad_hat - centre - x_hat * slope)
        out_ref[:, at] = out.astype(BF16)
    lane = lax.broadcasted_iota(jnp.int32, (channels, 128), 1)
    first = sums[pl.ds(0, channels), :]
    first = jnp.where(lane == 73, jnp.sum(gain_sum, axis=1, keepdims=True), first)
    first = jnp.where(lane == 74, jnp.sum(bias_sum, axis=1, keepdims=True), first)
    sums[pl.ds(0, channels), :] = first
    for i in range(3):
        rs = pl.ds(i * channels, channels)
        weight = dot(gp_ref[rs, :], normed_ref[...], NT)
        part_ref[rs, :] = weight[:, :128] / texels
        part_ref[pl.ds(width + i * channels, channels), :] = (weight[:, 128:] + sums[rs, :]) / texels
    part_ref[pl.ds(2 * width, part_rows - 2 * width), :] = jnp.zeros((part_rows - 2 * width, 128), F32)


def call(kernel, out_shape, args, in_specs=None, out_specs=None, scratch=()):
    return pl.pallas_call(
        kernel,
        out_shape=out_shape,
        in_specs=in_specs or [VMEM] * len(args),
        out_specs=out_specs or (VMEM,) * len(out_shape),
        scratch_shapes=scratch,
        compiler_params=pltpu.CompilerParams(vmem_limit_bytes=LIMIT),
    )(*args)


def constants(rows, cols):
    cells, wide = rows * cols, (rows + 2) * cols
    pick = np.zeros((2 * SIDE, cells), np.float32)
    shift = np.zeros((2, cols, cols), np.float32)
    spread = np.zeros((2, 3, SIDE, wide), np.float32)
    for y in range(rows):
        pick[y, y * cols] = 1.0
        pick[SIDE + y, y * cols + cols - 1] = 1.0
    for x in range(cols - 1):
        shift[0, x, x + 1] = 1.0
        shift[1, x + 1, x] = 1.0
    for side, col in ((0, 0), (1, cols - 1)):
        spread[side, 0, rows - 1, col] = 1.0
        for y in range(rows):
            spread[side, 1, y, (y + 1) * cols + col] = 1.0
        spread[side, 2, 0, (rows + 1) * cols + col] = 1.0
    return (
        jnp.asarray(pick, BF16),
        jnp.asarray(shift, BF16),
        jnp.asarray(spread.reshape(2, 3 * SIDE, wide), BF16),
    )


def body(x, g, gain, bias, weight, filter_taps, sharpness, out_matrix):
    channels, rows, cols = x.shape
    cells = rows * cols
    width = weight.shape[0]
    texels = float(cells * lax.axis_size("gy") * lax.axis_size("gx"))
    pick, shift, spread = constants(rows, cols)
    x = x.reshape(channels, cells)
    g = g.reshape(channels, cells)
    gain, bias = gain[:, None], bias[:, None]
    taps = filter_taps.reshape(9, width).T
    shape = jax.ShapeDtypeStruct

    p, normed, stat, edge = call(
        functools.partial(front_kernel, rows, cols),
        (shape((width, cells), BF16), shape((256, cells), BF16), shape((8, cells), F32),
         shape((2 * SIDE, width), BF16)),
        (x, gain, bias, weight, pick),
    )
    top, bot, side = halo(p, edge, cols, 0)
    moved = pltpu.VMEM((2, width, (rows + 2) * cols), BF16)
    conv, part = call(
        functools.partial(conv_kernel, rows, cols),
        (shape((width, cells), BF16), shape((padded_rows(2 * (channels + HD)), 128), F32)),
        (p, top, bot, side, shift, spread, taps, g),
        scratch=(moved, pltpu.VMEM((width, 128), F32)),
    )
    total = sum_over_devices(part, 1)
    grad, edge, omap_adj, sharp_adj = call(
        functools.partial(attend_kernel, texels),
        (shape((width, cells), BF16), shape((2 * SIDE, width), BF16),
         shape((channels, channels), F32), shape((ATTENDER_TOTAL,), F32)),
        (total, sharpness, out_matrix, conv, g, pick),
        in_specs=[VMEM, SMEM] + [VMEM] * 4,
        out_specs=(VMEM, VMEM, VMEM, SMEM),
    )
    top, bot, side = halo(grad, edge, cols, 2)
    out, part = call(
        functools.partial(back_kernel, rows, cols, texels),
        (shape((channels, cells), BF16), shape((padded_rows(2 * width), 128), F32)),
        (grad, top, bot, side, shift, spread, taps, p, normed, weight, x, stat, gain, g),
        scratch=(moved, pltpu.VMEM((width, cells), BF16), pltpu.VMEM((width, 128), F32)),
    )
    total = sum_over_devices(part, 3)
    low, high = total[:width], total[width:2 * width]
    weight_adj = jnp.concatenate([low, high[:, :channels - 128]], axis=1)
    filter_adj = high[:, 64:73].T.reshape(3, 3, width)
    return (
        out.reshape(channels, rows, cols),
        weight_adj,
        filter_adj,
        omap_adj,
        sharp_adj,
        high[:channels, 73],
        high[:channels, 74],
    )


def solution(mesh):
    in_specs = (P(None, "gy", "gx"), P(None, "gy", "gx"), P(), P(), P(), P(), P(), P())
    out_specs = (P(None, "gy", "gx"), P(), P(), P(), P(), P(), P())
    return jax.shard_map(body, mesh=mesh, in_specs=in_specs, out_specs=out_specs, check_vma=False)
```

time: 465 us -> 143 us (0.31)
  waiting for transfers between devices: 207 us -> 0 us
  Pallas kernels: 0 us -> 123 us
  local copies, waits for them, and re-layouts: 84.7 us -> 18.5 us
  other arithmetic: 66.2 us -> 0.82 us
  blocking collectives: 41.4 us -> 0 us
  matrix products: 24.9 us -> 0 us
  starting transfers between devices: 24 us -> 0 us
  between operations: 14.6 us -> 0.71 us
    psum x2 -> x0, waiting for transfers between devices: 207 us -> none  [the longest x1 124 us: body(): lax.psum((squares_q, squares_k, similarity_matrix), ('gy', 'gx'))]
    pallas_call x0 -> x8, Pallas kernels: none -> 123 us  [the longest x2 61.4 us: sum_over_devices(): pl.pallas_call(sum_kernel, out_shape=jax.ShapeDtypeStruct(shape, F32), in...]
    psum x1 -> x0, blocking collectives: 41.4 us -> none  [body(): depth_total = lax.psum(depth_term, ('gy', 'gx'))]
    convert_element_type x5 -> x0, other arithmetic: 30 us -> none  [the longest x1 11.7 us: body(): conv_out = conv_padded(padded, spatial_filter_taps, tile_rows, tile_cols)...]
    dot_general x11 -> x0, matrix products: 24.9 us -> none  [the longest x1 3.85 us: body(): jnp.einsum('hij,hin->hjn', plane_mixing_matrix, queries, preferred_elemen...]
    ppermute x8 -> x0, starting transfers between devices: 23.7 us -> none  [the longest x4 18.4 us: extended(): lax.ppermute(lax.slice_in_dim(block, block.shape[dim] - width, None, axis...]
    reduce_sum x7 -> x0, other arithmetic: 19.9 us -> none  [the longest x2 14.3 us: body(): tap_line.append(jnp.sum(grad_conv_f32 * window, axis=(1, 2)))]
    unnamed x85 -> x10, local copies, waits for them, and re-layouts: 28.2 us -> 8.99 us
  transfers between devices with their start and end apart: 10 -> 0, of which waited for: 2 -> 0; matrix products, arithmetic and copies ran while one was open for 12% -> 0% of each run, Pallas kernels for 0% -> 0%
where the time goes in v1:
time: 143 us
  Pallas kernels  123 us (86%)
  local copies, waits for them, and re-layouts  18.5 us (13%)
    pallas_call x2, Pallas kernels, sum_over_devices(): pl.pallas_call(sum_kernel, out_shape=jax.ShapeDtypeStruct(shape, F32), in...  61.4 us
    pallas_call x4, Pallas kernels, call(): pl.pallas_call(kernel, out_shape=out_shape, in_specs=in_specs or [VMEM] *...  44.8 us
    pallas_call x2, Pallas kernels, halo(): pl.pallas_call(functools.partial(halo_kernel, cols), out_shape=(jax.Shape...  16.6 us
    unnamed x10, local copies, waits for them, and re-layouts  8.99 us
    broadcast_in_dim x2, local copies, waits for them, and re-layouts, body(): gain, bias = (gain[:, None], bias[:, None])  2.88 us

profile of v1, /device:TPU:0, one launch (start us, length us, event | category | flops | bytes accessed | tf_op | source)
XLA Modules:
  0.0 142.9 jit_solution(2894965221851423176)
XLA Ops:
  0.6 0.8 reshape.42
  1.5 1.4 %copy.24.gain_ref = f32[192,1]{1,0:T(8,128)} copy(f32[192,1]{0,1:T(1,128)} %bitcast.35) | data formatting | bytes 1536 | tf_op jit(solution)/shard_map/broadcast_in_dim | solution.py:472
  2.9 1.4 %copy.25.bias_ref = f32[192,1]{1,0:T(8,128)} copy(f32[192,1]{0,1:T(1,128)} %bitcast.36) | data formatting | bytes 1536 | tf_op jit(solution)/shard_map/broadcast_in_dim | solution.py:472
  4.4 0.9 copy.27
  5.3 1.8 %copy.26.w_ref = bf16[576,192]{1,0:T(8,128)(2,1)} copy(bf16[576,192]{0,1:T(8,128)(2,1)} %param.15) | data formatting | bytes 442368 | tf_op args[4]
  7.1 2.2 %copy.39 = bf16[24,8,8,256]{3,1,2,0:T(8,128)(2,1)} copy(bf16[24,8,8,256]{3,2,1,0:T(8,128)(2,1)} %bitcast.29) | data formatting | bytes 1572864
  9.3 1.2 copy.40
  10.4 4.0 %shard_map.162 = (bf16[576,2048]{1,0:T(8,128)(2,1)}, bf16[256,2048]{1,0:T(8,128)(2,1)}, f32[8,2048]{1,0:T(8,128)}, bf16[32,576]{1,0:T(8,128)(2,1)}) custom-call(bf16[192,2048]{1,0:T(8,128)(2,1)} %bitcast.20, f32[192,1]{1,0:T(8,128)} %copy.24.gain_ref, f32[192,1]{1,0:T(8,128)} %copy.25.bias_ref, bf16[576,192]{1,0:T(8,128)(2,1)} %copy.26.w_ref, ...), custom_call_target="tpu_custom_call" | custom-call | tf_op jit(solution)/shard_map/pallas_call | solution.py:431
  14.5 9.5 %shard_map.163 = (bf16[576,256]{1,0:T(8,128)(2,1)}, bf16[576,256]{1,0:T(8,128)(2,1)}, bf16[2,3,16,576]{3,2,1,0:T(8,128)(2,1)}) custom-call(bf16[576,2048]{1,0:T(8,128)(2,1)} %get-tuple-element.25.p_ref, bf16[32,576]{1,0:T(8,128)(2,1)} %get-tuple-element.26.edge_ref), custom_call_target="tpu_custom_call" | custom-call | tf_op jit(solution)/shard_map/pallas_call | solution.py:128
  24.0 15.8 %shard_map.164 = (bf16[576,2048]{1,0:T(8,128)(2,1)}, f32[512,128]{1,0:T(8,128)}) custom-call(bf16[576,2048]{1,0:T(8,128)(2,1)} %get-tuple-element.25.p_ref, bf16[576,256]{1,0:T(8,128)(2,1)} %get-tuple-element.27.top_ref, bf16[576,256]{1,0:T(8,128)(2,1)} %get-tuple-element.28.bot_ref, bf16[2,3,16,576]{3,2,1,0:T(8,128)(2,1)} %get-tuple-element.29.side_ref, ...), custom_call_target="tpu_custom_call" | custom-call | tf_op jit(solution)/shard_map/pallas_call | solution.py:431
  39.7 26.7 %shard_map.165 = f32[4,8,16,128]{3,2,1,0:T(8,128)} custom-call(f32[4,8,16,128]{3,2,1,0:T(8,128)} %bitcast.34), custom_call_target="tpu_custom_call" | custom-call | tf_op jit(solution)/shard_map/pallas_call | solution.py:273
  66.4 6.6 %shard_map.166 = (bf16[576,2048]{1,0:T(8,128)(2,1)}, bf16[32,576]{1,0:T(8,128)(2,1)}, f32[192,192]{1,0:T(8,128)}, f32[4]{0:T(128)}) custom-call(f32[512,128]{1,0:T(8,128)} %bitcast.28, f32[4]{0:T(128)} %sharp_ref.1, bf16[192,192]{1,0:T(8,128)(2,1)} %wo_ref.1, bf16[576,2048]{1,0:T(8,128)(2,1)} %get-tuple-element.31.conv_ref, bf16[192,2048]{1,0:T(8,128)(2,1)} %bitcast.18, ...), custom_call_target="tpu_custom_call" | custom-call | tf_op jit(solution)/shard_map/pallas_call | solution.py:431
  73.1 7.1 %shard_map.167 = (bf16[576,256]{1,0:T(8,128)(2,1)}, bf16[576,256]{1,0:T(8,128)(2,1)}, bf16[2,3,16,576]{3,2,1,0:T(8,128)(2,1)}) custom-call(bf16[576,2048]{1,0:T(8,128)(2,1)} %get-tuple-element.32.p_ref.grad_ref, bf16[32,576]{1,0:T(8,128)(2,1)} %get-tuple-element.33.edge_ref), custom_call_target="tpu_custom_call" | custom-call | tf_op jit(solution)/shard_map/pallas_call | solution.py:128
  80.1 18.4 %shard_map.168 = (bf16[192,2048]{1,0:T(8,128)(2,1)}, f32[1280,128]{1,0:T(8,128)}) custom-call(bf16[576,2048]{1,0:T(8,128)(2,1)} %get-tuple-element.32.p_ref.grad_ref, bf16[576,256]{1,0:T(8,128)(2,1)} %get-tuple-element.34.top_ref, bf16[576,256]{1,0:T(8,128)(2,1)} %get-tuple-element.35.bot_ref, bf16[2,3,16,576]{3,2,1,0:T(8,128)(2,1)} %get-tuple-element.36.side_ref, ...), custom_call_target="tpu_custom_call" | custom-call | tf_op jit(solution)/shard_map/pallas_call | solution.py:431
  98.6 2.2 %copy.41 = bf16[24,8,8,256]{3,2,1,0:T(8,128)(2,1)} copy(bf16[24,8,8,256]{3,1,2,0:T(8,128)(2,1)} %bitcast.32) | data formatting | bytes 1572864
  100.8 34.7 %shard_map.169 = f32[4,8,40,128]{3,2,1,0:T(8,128)} custom-call(f32[4,8,40,128]{3,2,1,0:T(8,128)} %bitcast.33), custom_call_target="tpu_custom_call" | custom-call | tf_op jit(solution)/shard_map/pallas_call | solution.py:273
  135.5 1.1 fusion
  136.6 0.6 copy.38
  137.2 0.6 copy.37
  137.9 1.0 slice.26
  139.0 1.0 slice.25
  140.0 1.1 slice_bitcast_fusion
  141.2 0.7 reshape.49
  142.0 0.8 pad_maximum_fusion
  (5 shorter events, 0.4 us)
Async XLA Ops:
  0.6 8.7 %copy-start = (bf16[192,8,256]{2,1,0:T(8,128)(2,1)S(1)}, bf16[192,8,256]{2,1,0:T(8,128)(2,1)}, u32[]{:S(2)}) copy-start(bf16[192,8,256]{2,1,0:T(8,128)(2,1)} %param.12) | copy-start | bytes 2359300

commit v2 on v1

--- a/solution.py
+++ b/solution.py
@@ -31,15 +31,20 @@
     )
 
 
-def front_kernel(rows, cols, x_ref, gain_ref, bias_ref, w_ref, sel_ref,
+def to_col(row):
+    size = row.shape[1]
+    eye = lax.broadcasted_iota(jnp.int32, (size, size), 0) == lax.broadcasted_iota(
+        jnp.int32, (size, size), 1
+    )
+    return jnp.sum(jnp.where(eye, row, 0.0), axis=1, keepdims=True)
+
+
+def front_kernel(rows, cols, x_ref, gain_ref, bias_ref, wt_ref, sel_ref,
                  p_ref, normed_ref, stat_ref, edge_ref):
     channels = x_ref.shape[0]
-    gain = gain_ref[...]
-    bias = bias_ref[...]
+    gain, bias = to_col(gain_ref[...]), to_col(bias_ref[...])
+    weight = jnp.transpose(wt_ref[...])
     edge = jnp.zeros((2 * SIDE, channels), F32)
-    normed_ref[pl.ds(channels, normed_ref.shape[0] - channels), :] = jnp.zeros(
-        (normed_ref.shape[0] - channels, rows * cols), BF16
-    )
     stat_ref[...] = jnp.zeros_like(stat_ref)
     for y in range(rows):
         at = pl.ds(y * cols, cols)
@@ -51,10 +56,10 @@
         stat_ref[pl.ds(0, 1), at] = mean
         stat_ref[pl.ds(1, 1), at] = inv
         normed = ((centred * inv) * gain + bias).astype(BF16)
-        normed_ref[pl.ds(0, channels), at] = normed
-        p_ref[:, at] = dot(w_ref[...], normed).astype(BF16)
+        normed_ref[:, at] = normed
+        p_ref[:, at] = dot(weight, normed).astype(BF16)
         edge = edge + dot(sel_ref[:, at], normed, NT)
-    edge_ref[...] = dot(edge.astype(BF16), w_ref[...], NT).astype(BF16)
+    edge_ref[...] = dot(edge.astype(BF16), wt_ref[...]).astype(BF16)
 
 
 def halo_kernel(cols, p_ref, edge_ref, top_ref, bot_ref, side_ref, send, recv):
@@ -143,8 +148,8 @@
 
 def shift_rows(rows, cols, p_ref, top_ref, bot_ref, side_ref, shift_ref, spread_ref, moved):
     width = p_ref.shape[0]
+    edges = [jnp.transpose(side_ref[side].reshape(3 * SIDE, width)) for side in range(2)]
     for y in range(rows + 2):
-        at = pl.ds(y * cols, cols)
         if y == 0:
             row = top_ref[...]
         elif y == rows + 1:
@@ -152,9 +157,13 @@
         else:
             row = p_ref[:, pl.ds((y - 1) * cols, cols)]
         for side in range(2):
-            edge = side_ref[side].reshape(3 * SIDE, width)
-            fill = dot(edge, spread_ref[side, :, at], TN)
-            moved[side, :, at] = (dot(row, shift_ref[side]) + fill).astype(BF16)
+            near, far = (0, 128) if side == 0 else (cols - 128, 0)
+            out = dot(row, shift_ref[side])
+            at = pl.ds(y * cols + near, 128)
+            fill = dot(edges[side], spread_ref[side, :, at])
+            moved[side, :, at] = (out[:, near:near + 128] + fill).astype(BF16)
+            rest = cols - 128
+            moved[side, :, pl.ds(y * cols + far, rest)] = out[:, far:far + rest].astype(BF16)
 
 
 def conv_kernel(rows, cols, p_ref, top_ref, bot_ref, side_ref, shift_ref, spread_ref, taps_ref,
@@ -216,7 +225,8 @@
     part_ref[pl.ds(2 * span, part_rows - 2 * span), :] = jnp.zeros((part_rows - 2 * span, 128), F32)
 
 
-def sum_kernel(in_ref, out_ref, got_x, held, got_y, send, recv):
+def sum_kernel(finish, in_ref, *refs):
+    results, (out_ref, got_x, held, got_y, send, recv) = refs[:-6], refs[-6:]
     gy, gx = lax.axis_index("gy"), lax.axis_index("gx")
     ny, nx = lax.axis_size("gy"), lax.axis_size("gx")
     barrier = pltpu.get_barrier_semaphore()
@@ -245,40 +255,63 @@
         (in_ref.at[lax.rem(gx + d, nx)], got_x.at[d - 1], (gy, lax.rem(gx + d, nx)))
         for d in range(1, nx)
     ])
-    total = in_ref[gx]
+    total = in_ref[gx].astype(F32)
     for d in range(1, nx):
-        total = total + got_x[d - 1]
-    held[...] = total
+        total = total + got_x[d - 1].astype(F32)
+    held[...] = total.astype(held.dtype)
     exchange([
         (held.at[lax.rem(gy + d, ny)], got_y.at[d - 1], (lax.rem(gy + d, ny), gx))
         for d in range(1, ny)
     ])
-    total = held[gy]
+    total = held[gy].astype(F32)
     for d in range(1, ny):
-        total = total + got_y[d - 1]
-    out_ref[gx, gy] = total
+        total = total + got_y[d - 1].astype(F32)
+    out_ref[gx, gy] = total.astype(out_ref.dtype)
     exchange([
         (out_ref.at[gx, gy], out_ref.at[gx, gy], (lax.rem(gy + d, ny), gx)) for d in range(1, ny)
     ])
     exchange([
         (out_ref.at[gx], out_ref.at[gx], (gy, lax.rem(gx + d, nx))) for d in range(1, nx)
     ])
-
-
-def sum_over_devices(part, collective_id):
+    finish(out_ref[...].reshape(-1, 128), *results)
+
+
+def whole_sum(total, out_ref):
+    out_ref[...] = total
+
+
+def parameter_sums(total, weight_ref, taps_ref, gain_ref, bias_ref):
+    total = total.astype(F32)
+    channels, width = weight_ref.shape
+    whole, half, at = width // 128, channels // 2, 0
+    for i in range(whole):
+        weight_ref[:, pl.ds(i * 128, 128)] = total[at:at + channels]
+        at += channels
+    rest = total[at:at + half]
+    left = width - whole * 128
+    weight_ref[:, pl.ds(whole * 128, left)] = jnp.concatenate([rest[:, :left], rest[:, left:]], axis=0)
+    at += half
+    small = jnp.concatenate([total[at + 16 * i:at + 16 * i + 16] for i in range(whole + 1)], axis=1)
+    taps_ref[...] = small[:9, :width]
+    gain_ref[...] = small[9:10, :channels]
+    bias_ref[...] = small[10:11, :channels]
+
+
+def sum_over_devices(part, collective_id, finish, out_shape):
     ny, nx = lax.axis_size("gy"), lax.axis_size("gx")
     piece = part.shape[0] // (nx * ny)
     count = 2 * (nx + ny - 2)
     shape = (nx, ny, piece, 128)
-    out = pl.pallas_call(
-        sum_kernel,
-        out_shape=jax.ShapeDtypeStruct(shape, F32),
+    return pl.pallas_call(
+        functools.partial(sum_kernel, finish),
+        out_shape=out_shape,
         in_specs=[VMEM],
-        out_specs=VMEM,
+        out_specs=(VMEM,) * len(out_shape),
         scratch_shapes=[
-            pltpu.VMEM((nx - 1, ny, piece, 128), F32),
-            pltpu.VMEM((ny, piece, 128), F32),
-            pltpu.VMEM((ny - 1, piece, 128), F32),
+            pltpu.VMEM(shape, part.dtype),
+            pltpu.VMEM((nx - 1, ny, piece, 128), part.dtype),
+            pltpu.VMEM((ny, piece, 128), part.dtype),
+            pltpu.VMEM((ny - 1, piece, 128), part.dtype),
             pltpu.SemaphoreType.DMA((count,)),
             pltpu.SemaphoreType.DMA((count,)),
         ],
@@ -286,11 +319,10 @@
             collective_id=collective_id, has_side_effects=True, vmem_limit_bytes=LIMIT
         ),
     )(part.reshape(shape))
-    return out.reshape(part.shape)
-
-
-def padded_rows(count):
-    unit = 8 * lax.axis_size("gy") * lax.axis_size("gx")
+
+
+def padded_rows(count, tile=8):
+    unit = tile * lax.axis_size("gy") * lax.axis_size("gx")
     return -(-count // unit) * unit
 
 
@@ -318,9 +350,6 @@
 
     def to_row(col):
         return jnp.sum(jnp.where(eye, col, 0.0), axis=0, keepdims=True)
-
-    def to_col(row):
-        return jnp.sum(jnp.where(eye, row, 0.0), axis=1, keepdims=True)
 
     norms = jnp.sqrt(sq + 1e-06) * jnp.sqrt(to_row(sk) + 1e-06)
     logits = jnp.where(same, sharp * gram / norms, 0.0)
@@ -359,7 +388,7 @@
 
 
 def back_kernel(rows, cols, texels, grad_ref, top_ref, bot_ref, side_ref, shift_ref, spread_ref,
-                taps_ref, p_ref, normed_ref, w_ref, x_ref, stat_ref, gain_ref, g_ref,
+                taps_ref, p_ref, normed_ref, wt_ref, x_ref, stat_ref, gain_ref, g_ref,
                 out_ref, part_ref, moved, gp_ref, sums):
     width = grad_ref.shape[0]
     channels = width // 3
@@ -394,17 +423,17 @@
         lane = lax.broadcasted_iota(jnp.int32, (16, 128), 1)
         packed = jnp.zeros((16, 128), F32)
         for k in range(9):
-            packed = jnp.where(lane == 64 + k, jnp.sum(tap_sums[k], axis=1, keepdims=True), packed)
+            packed = jnp.where(lane == k, jnp.sum(tap_sums[k], axis=1, keepdims=True), packed)
         sums[rs, :] = packed
         return carry
 
     lax.fori_loop(0, width // 16, chunk, 0)
-    gain = gain_ref[...]
+    gain = to_col(gain_ref[...])
     gain_sum = jnp.zeros((channels, cols), F32)
     bias_sum = jnp.zeros((channels, cols), F32)
     for y in range(rows):
         at = pl.ds(y * cols, cols)
-        grad_normed = dot(w_ref[...], gp_ref[:, at], TN)
+        grad_normed = dot(wt_ref[...], gp_ref[:, at])
         mean, inv = stat_ref[pl.ds(0, 1), at], stat_ref[pl.ds(1, 1), at]
         x_hat = (x_ref[:, at].astype(F32) - mean) * inv
         gain_sum = gain_sum + grad_normed * x_hat
@@ -416,15 +445,23 @@
         out_ref[:, at] = out.astype(BF16)
     lane = lax.broadcasted_iota(jnp.int32, (channels, 128), 1)
     first = sums[pl.ds(0, channels), :]
-    first = jnp.where(lane == 73, jnp.sum(gain_sum, axis=1, keepdims=True), first)
-    first = jnp.where(lane == 74, jnp.sum(bias_sum, axis=1, keepdims=True), first)
+    first = jnp.where(lane == 9, jnp.sum(gain_sum, axis=1, keepdims=True), first)
+    first = jnp.where(lane == 10, jnp.sum(bias_sum, axis=1, keepdims=True), first)
     sums[pl.ds(0, channels), :] = first
-    for i in range(3):
-        rs = pl.ds(i * channels, channels)
-        weight = dot(gp_ref[rs, :], normed_ref[...], NT)
-        part_ref[rs, :] = weight[:, :128] / texels
-        part_ref[pl.ds(width + i * channels, channels), :] = (weight[:, 128:] + sums[rs, :]) / texels
-    part_ref[pl.ds(2 * width, part_rows - 2 * width), :] = jnp.zeros((part_rows - 2 * width, 128), F32)
+    sums[pl.ds(width, 64), :] = jnp.zeros((64, 128), F32)
+    weight = dot(normed_ref[...], gp_ref[...], NT) / texels
+    whole, half, at = width // 128, channels // 2, 0
+    for i in range(whole):
+        part_ref[pl.ds(at, channels), :] = weight[:, i * 128:(i + 1) * 128].astype(BF16)
+        at += channels
+    rest = weight[:, whole * 128:]
+    part_ref[pl.ds(at, half), :] = jnp.concatenate([rest[:half], rest[half:]], axis=1).astype(BF16)
+    at += half
+    for i in range(whole + 1):
+        block = jnp.transpose(sums[pl.ds(i * 128, 128), :])[:16]
+        part_ref[pl.ds(at, 16), :] = (block / texels).astype(BF16)
+        at += 16
+    part_ref[pl.ds(at, part_rows - at), :] = jnp.zeros((part_rows - at, 128), BF16)
 
 
 def call(kernel, out_shape, args, in_specs=None, out_specs=None, scratch=()):
@@ -469,15 +506,15 @@
     pick, shift, spread = constants(rows, cols)
     x = x.reshape(channels, cells)
     g = g.reshape(channels, cells)
-    gain, bias = gain[:, None], bias[:, None]
+    gain, bias, weight_t = gain[None, :], bias[None, :], weight.T
     taps = filter_taps.reshape(9, width).T
     shape = jax.ShapeDtypeStruct
 
     p, normed, stat, edge = call(
         functools.partial(front_kernel, rows, cols),
-        (shape((width, cells), BF16), shape((256, cells), BF16), shape((8, cells), F32),
+        (shape((width, cells), BF16), shape((channels, cells), BF16), shape((8, cells), F32),
          shape((2 * SIDE, width), BF16)),
-        (x, gain, bias, weight, pick),
+        (x, gain, bias, weight_t, pick),
     )
     top, bot, side = halo(p, edge, cols, 0)
     moved = pltpu.VMEM((2, width, (rows + 2) * cols), BF16)
@@ -487,7 +524,7 @@
         (p, top, bot, side, shift, spread, taps, g),
         scratch=(moved, pltpu.VMEM((width, 128), F32)),
     )
-    total = sum_over_devices(part, 1)
+    (total,) = sum_over_devices(part, 1, whole_sum, (shape(part.shape, F32),))
     grad, edge, omap_adj, sharp_adj = call(
         functools.partial(attend_kernel, texels),
         (shape((width, cells), BF16), shape((2 * SIDE, width), BF16),
@@ -497,24 +534,26 @@
         out_specs=(VMEM, VMEM, VMEM, SMEM),
     )
     top, bot, side = halo(grad, edge, cols, 2)
+    part_rows = width // 128 * channels + channels // 2 + (width // 128 + 1) * 16
     out, part = call(
         functools.partial(back_kernel, rows, cols, texels),
-        (shape((channels, cells), BF16), shape((padded_rows(2 * width), 128), F32)),
-        (grad, top, bot, side, shift, spread, taps, p, normed, weight, x, stat, gain, g),
-        scratch=(moved, pltpu.VMEM((width, cells), BF16), pltpu.VMEM((width, 128), F32)),
-    )
-    total = sum_over_devices(part, 3)
-    low, high = total[:width], total[width:2 * width]
-    weight_adj = jnp.concatenate([low, high[:, :channels - 128]], axis=1)
-    filter_adj = high[:, 64:73].T.reshape(3, 3, width)
+        (shape((channels, cells), BF16), shape((padded_rows(part_rows, 16), 128), BF16)),
+        (grad, top, bot, side, shift, spread, taps, p, normed, weight_t, x, stat, gain, g),
+        scratch=(moved, pltpu.VMEM((width, cells), BF16), pltpu.VMEM((width + 64, 128), F32)),
+    )
+    weight_adj, filter_adj, gain_adj, bias_adj = sum_over_devices(
+        part, 3, parameter_sums,
+        (shape((channels, width), F32), shape((9, width), F32),
+         shape((1, channels), F32), shape((1, channels), F32)),
+    )
     return (
         out.reshape(channels, rows, cols),
-        weight_adj,
-        filter_adj,
+        weight_adj.T,
+        filter_adj.reshape(3, 3, width),
         omap_adj,
         sharp_adj,
-        high[:channels, 73],
-        high[:channels, 74],
+        gain_adj.reshape(channels),
+        bias_adj.reshape(channels),
     )
 
 

time: 143 us -> 125 us (0.87)
  Pallas kernels: 123 us -> 110 us
  local copies, waits for them, and re-layouts: 18.5 us -> 13 us
    pallas_call x2, Pallas kernels: 61.4 us -> 51.1 us  [sum_over_devices(): pl.pallas_call(functools.partial(sum_kernel, finish), out_shape=out_shape...]
    slice x3 -> x0, local copies, waits for them, and re-layouts: 3.05 us -> none  [the longest x1 1.08 us: body(): high[:channels, 74]]
    broadcast_in_dim x2 -> x0, local copies, waits for them, and re-layouts: 2.88 us -> none  [body(): gain, bias = (gain[:, None], bias[:, None])]
    pallas_call x4, Pallas kernels: 44.8 us -> 42.7 us  [call(): pl.pallas_call(kernel, out_shape=out_shape, in_specs=in_specs or [VMEM] *...]
    unnamed x10 -> x8, local copies, waits for them, and re-layouts: 8.99 us -> 9.85 us
where the time goes in v2:
time: 125 us; the launch traced here: 124 us
  Pallas kernels  110 us (88%)
  local copies, waits for them, and re-layouts  13 us (10%)
    pallas_call x2, Pallas kernels, sum_over_devices(): pl.pallas_call(functools.partial(sum_kernel, finish), out_shape=out_shape...  51.1 us
    pallas_call x4, Pallas kernels, call(): pl.pallas_call(kernel, out_shape=out_shape, in_specs=in_specs or [VMEM] *...  42.7 us
    pallas_call x2, Pallas kernels, halo(): pl.pallas_call(functools.partial(halo_kernel, cols), out_shape=(jax.Shape...  16.6 us
    unnamed x8, local copies, waits for them, and re-layouts  9.85 us

profile of v2, /device:TPU:0, one launch (start us, length us, event | category | flops | bytes accessed | tf_op | source)
XLA Modules:
  0.0 124.0 jit_solution(4412452918034922745)
XLA Ops:
  0.6 0.0 copy-start
  0.6 0.8 reshape.42
  1.5 0.9 copy.19
  2.4 2.2 %copy.20 = bf16[24,8,8,256]{3,1,2,0:T(8,128)(2,1)} copy(bf16[24,8,8,256]{3,2,1,0:T(8,128)(2,1)} %bitcast.24) | data formatting | bytes 1572864
  4.6 0.0 copy-done
  4.6 1.2 copy.21
  5.8 4.0 %shard_map.162 = (bf16[576,2048]{1,0:T(8,128)(2,1)}, bf16[192,2048]{1,0:T(8,128)(2,1)}, f32[8,2048]{1,0:T(8,128)}, bf16[32,576]{1,0:T(8,128)(2,1)}) custom-call(bf16[192,2048]{1,0:T(8,128)(2,1)} %bitcast.18, f32[1,192]{1,0:T(1,128)} %bitcast.31, f32[1,192]{1,0:T(1,128)} %bitcast.33, bf16[192,576]{1,0:T(8,128)(2,1)} %bitcast.22, ...), custom_call_target="tpu_custom_call" | custom-call | tf_op jit(solution)/shard_map/pallas_call | solution.py:468
  9.8 9.5 %shard_map.163 = (bf16[576,256]{1,0:T(8,128)(2,1)}, bf16[576,256]{1,0:T(8,128)(2,1)}, bf16[2,3,16,576]{3,2,1,0:T(8,128)(2,1)}) custom-call(bf16[576,2048]{1,0:T(8,128)(2,1)} %get-tuple-element.29.p_ref, bf16[32,576]{1,0:T(8,128)(2,1)} %get-tuple-element.30.edge_ref), custom_call_target="tpu_custom_call" | custom-call | tf_op jit(solution)/shard_map/pallas_call | solution.py:133
  19.2 15.0 %shard_map.164 = (bf16[576,2048]{1,0:T(8,128)(2,1)}, f32[512,128]{1,0:T(8,128)}) custom-call(bf16[576,2048]{1,0:T(8,128)(2,1)} %get-tuple-element.29.p_ref, bf16[576,256]{1,0:T(8,128)(2,1)} %get-tuple-element.31.top_ref, bf16[576,256]{1,0:T(8,128)(2,1)} %get-tuple-element.32.bot_ref, bf16[2,3,16,576]{3,2,1,0:T(8,128)(2,1)} %get-tuple-element.33.side_ref, ...), custom_call_target="tpu_custom_call" | custom-call | tf_op jit(solution)/shard_map/pallas_call | solution.py:468
  34.2 26.7 %shard_map.165.tot_ref = f32[512,128]{1,0:T(8,128)} custom-call(f32[4,8,16,128]{3,2,1,0:T(8,128)} %bitcast.30), custom_call_target="tpu_custom_call" | custom-call | tf_op jit(solution)/shard_map/pallas_call | solution.py:305
  60.9 6.6 %shard_map.166 = (bf16[576,2048]{1,0:T(8,128)(2,1)}, bf16[32,576]{1,0:T(8,128)(2,1)}, f32[192,192]{1,0:T(8,128)}, f32[4]{0:T(128)}) custom-call(f32[512,128]{1,0:T(8,128)} %shard_map.165.tot_ref, f32[4]{0:T(128)} %sharp_ref.1, bf16[192,192]{1,0:T(8,128)(2,1)} %wo_ref.1, bf16[576,2048]{1,0:T(8,128)(2,1)} %get-tuple-element.35.conv_ref, ...), custom_call_target="tpu_custom_call" | custom-call | tf_op jit(solution)/shard_map/pallas_call | solution.py:468
  67.6 7.1 %shard_map.167 = (bf16[576,256]{1,0:T(8,128)(2,1)}, bf16[576,256]{1,0:T(8,128)(2,1)}, bf16[2,3,16,576]{3,2,1,0:T(8,128)(2,1)}) custom-call(bf16[576,2048]{1,0:T(8,128)(2,1)} %get-tuple-element.36.p_ref.grad_ref, bf16[32,576]{1,0:T(8,128)(2,1)} %get-tuple-element.37.edge_ref), custom_call_target="tpu_custom_call" | custom-call | tf_op jit(solution)/shard_map/pallas_call | solution.py:133
  74.7 17.1 %shard_map.168 = (bf16[192,2048]{1,0:T(8,128)(2,1)}, bf16[1024,128]{1,0:T(8,128)(2,1)}) custom-call(bf16[576,2048]{1,0:T(8,128)(2,1)} %get-tuple-element.36.p_ref.grad_ref, bf16[576,256]{1,0:T(8,128)(2,1)} %get-tuple-element.38.top_ref, bf16[576,256]{1,0:T(8,128)(2,1)} %get-tuple-element.39.bot_ref, bf16[2,3,16,576]{3,2,1,0:T(8,128)(2,1)} %get-tuple-element.40.side_ref, ...), custom_call_target="tpu_custom_call" | custom-call | tf_op jit(solution)/shard_map/pallas_call | solution.py:468
  91.8 2.2 %copy.22 = bf16[24,8,8,256]{3,2,1,0:T(8,128)(2,1)} copy(bf16[24,8,8,256]{3,1,2,0:T(8,128)(2,1)} %bitcast.27) | data formatting | bytes 1572864
  94.0 24.4 %shard_map.169 = (f32[192,576]{1,0:T(8,128)}, f32[9,576]{1,0:T(8,128)}, f32[1,192]{1,0:T(1,128)}, f32[1,192]{1,0:T(1,128)}) custom-call(bf16[4,8,32,128]{3,2,1,0:T(8,128)(2,1)} %bitcast.29), custom_call_target="tpu_custom_call" | custom-call | tf_op jit(solution)/shard_map/pallas_call | solution.py:305
  118.4 1.4 %reshape.47 = f32[3,3,576]{2,1,0:T(4,128)} reshape(f32[9,576]{1,0:T(8,128)} %get-tuple-element.46) | data formatting | bytes 41472 | tf_op jit(solution)/shard_map/reshape | solution.py:552
  119.8 1.8 %copy.26 = f32[576,192]{0,1:T(8,128)} copy(f32[576,192]{0,1:T(8,128)} %bitcast.28) | data formatting | bytes 884736
  121.6 1.2 copy.27
  122.8 1.2 copy.28
Async XLA Ops:
  0.6 3.9 %copy-start = (bf16[192,8,256]{2,1,0:T(8,128)(2,1)S(1)}, bf16[192,8,256]{2,1,0:T(8,128)(2,1)}, u32[]{:S(2)}) copy-start(bf16[192,8,256]{2,1,0:T(8,128)(2,1)} %param.12) | copy-start | bytes 2359300

commit v3 on v2

--- a/solution.py
+++ b/solution.py
@@ -280,8 +280,8 @@
     out_ref[...] = total
 
 
-def parameter_sums(total, weight_ref, taps_ref, gain_ref, bias_ref):
-    total = total.astype(F32)
+def parameter_kernel(total_ref, weight_ref, taps_ref, gain_ref, bias_ref):
+    total = total_ref[...].astype(F32)
     channels, width = weight_ref.shape
     whole, half, at = width // 128, channels // 2, 0
     for i in range(whole):
@@ -292,7 +292,8 @@
     weight_ref[:, pl.ds(whole * 128, left)] = jnp.concatenate([rest[:, :left], rest[:, left:]], axis=0)
     at += half
     small = jnp.concatenate([total[at + 16 * i:at + 16 * i + 16] for i in range(whole + 1)], axis=1)
-    taps_ref[...] = small[:9, :width]
+    for a in range(3):
+        taps_ref[a] = small[3 * a:3 * a + 3, :width]
     gain_ref[...] = small[9:10, :channels]
     bias_ref[...] = small[10:11, :channels]
 
@@ -541,15 +542,17 @@
         (grad, top, bot, side, shift, spread, taps, p, normed, weight_t, x, stat, gain, g),
         scratch=(moved, pltpu.VMEM((width, cells), BF16), pltpu.VMEM((width + 64, 128), F32)),
     )
-    weight_adj, filter_adj, gain_adj, bias_adj = sum_over_devices(
-        part, 3, parameter_sums,
-        (shape((channels, width), F32), shape((9, width), F32),
+    (total,) = sum_over_devices(part, 3, whole_sum, (shape(part.shape, BF16),))
+    weight_adj, filter_adj, gain_adj, bias_adj = call(
+        parameter_kernel,
+        (shape((channels, width), F32), shape((3, 3, width), F32),
          shape((1, channels), F32), shape((1, channels), F32)),
+        (total,),
     )
     return (
         out.reshape(channels, rows, cols),
         weight_adj.T,
-        filter_adj.reshape(3, 3, width),
+        filter_adj,
         omap_adj,
         sharp_adj,
         gain_adj.reshape(channels),

time: 125 us -> 120 us (0.960)
  local copies, waits for them, and re-layouts: 13 us -> 7.32 us
  Pallas kernels: 110 us -> 112 us
    unnamed x8 -> x5, local copies, waits for them, and re-layouts: 9.85 us -> 5.6 us
    pallas_call x4 -> x5, Pallas kernels: 42.7 us -> 44.5 us  [call(): pl.pallas_call(kernel, out_shape=out_shape, in_specs=in_specs or [VMEM] *...]
    reshape x1 -> x0, local copies, waits for them, and re-layouts: 1.4 us -> none  [body(): filter_adj.reshape(3, 3, width)]
where the time goes in v3:
time: 120 us
  Pallas kernels  112 us (93%)
  local copies, waits for them, and re-layouts  7.32 us (6%)
    pallas_call x2, Pallas kernels, sum_over_devices(): pl.pallas_call(functools.partial(sum_kernel, finish), out_shape=out_shape...  50.9 us
    pallas_call x5, Pallas kernels, call(): pl.pallas_call(kernel, out_shape=out_shape, in_specs=in_specs or [VMEM] *...  44.5 us
    pallas_call x2, Pallas kernels, halo(): pl.pallas_call(functools.partial(halo_kernel, cols), out_shape=(jax.Shape...  16.6 us
    unnamed x5, local copies, waits for them, and re-layouts  5.6 us

profile of v3, /device:TPU:0, one launch (start us, length us, event | category | flops | bytes accessed | tf_op | source)
XLA Modules:
  0.0 120.0 jit_solution(14208130615364824210)
XLA Ops:
  0.6 0.0 copy-start
  0.6 0.8 reshape.39
  1.5 0.9 copy.19
  2.4 2.2 %copy.20 = bf16[24,8,8,256]{3,1,2,0:T(8,128)(2,1)} copy(bf16[24,8,8,256]{3,2,1,0:T(8,128)(2,1)} %bitcast.24) | data formatting | bytes 1572864
  4.6 0.0 copy-done
  4.6 1.2 copy.21
  5.8 4.0 %shard_map.162 = (bf16[576,2048]{1,0:T(8,128)(2,1)}, bf16[192,2048]{1,0:T(8,128)(2,1)}, f32[8,2048]{1,0:T(8,128)}, bf16[32,576]{1,0:T(8,128)(2,1)}) custom-call(bf16[192,2048]{1,0:T(8,128)(2,1)} %bitcast.18, f32[1,192]{1,0:T(1,128)} %bitcast.30, f32[1,192]{1,0:T(1,128)} %bitcast.32, bf16[192,576]{1,0:T(8,128)(2,1)} %bitcast.22, ...), custom_call_target="tpu_custom_call" | custom-call | tf_op jit(solution)/shard_map/pallas_call | solution.py:469
  9.8 9.5 %shard_map.163 = (bf16[576,256]{1,0:T(8,128)(2,1)}, bf16[576,256]{1,0:T(8,128)(2,1)}, bf16[2,3,16,576]{3,2,1,0:T(8,128)(2,1)}) custom-call(bf16[576,2048]{1,0:T(8,128)(2,1)} %get-tuple-element.29.p_ref, bf16[32,576]{1,0:T(8,128)(2,1)} %get-tuple-element.30.edge_ref), custom_call_target="tpu_custom_call" | custom-call | tf_op jit(solution)/shard_map/pallas_call | solution.py:133
  19.2 15.0 %shard_map.164 = (bf16[576,2048]{1,0:T(8,128)(2,1)}, f32[512,128]{1,0:T(8,128)}) custom-call(bf16[576,2048]{1,0:T(8,128)(2,1)} %get-tuple-element.29.p_ref, bf16[576,256]{1,0:T(8,128)(2,1)} %get-tuple-element.31.top_ref, bf16[576,256]{1,0:T(8,128)(2,1)} %get-tuple-element.32.bot_ref, bf16[2,3,16,576]{3,2,1,0:T(8,128)(2,1)} %get-tuple-element.33.side_ref, ...), custom_call_target="tpu_custom_call" | custom-call | tf_op jit(solution)/shard_map/pallas_call | solution.py:469
  34.2 26.7 %shard_map.165.tot_ref = f32[512,128]{1,0:T(8,128)} custom-call(f32[4,8,16,128]{3,2,1,0:T(8,128)} %bitcast.29), custom_call_target="tpu_custom_call" | custom-call | tf_op jit(solution)/shard_map/pallas_call | solution.py:306
  60.9 6.6 %shard_map.166 = (bf16[576,2048]{1,0:T(8,128)(2,1)}, bf16[32,576]{1,0:T(8,128)(2,1)}, f32[192,192]{1,0:T(8,128)}, f32[4]{0:T(128)}) custom-call(f32[512,128]{1,0:T(8,128)} %shard_map.165.tot_ref, f32[4]{0:T(128)} %sharp_ref.1, bf16[192,192]{1,0:T(8,128)(2,1)} %wo_ref.1, bf16[576,2048]{1,0:T(8,128)(2,1)} %get-tuple-element.35.conv_ref, ...), custom_call_target="tpu_custom_call" | custom-call | tf_op jit(solution)/shard_map/pallas_call | solution.py:469
  67.6 7.1 %shard_map.167 = (bf16[576,256]{1,0:T(8,128)(2,1)}, bf16[576,256]{1,0:T(8,128)(2,1)}, bf16[2,3,16,576]{3,2,1,0:T(8,128)(2,1)}) custom-call(bf16[576,2048]{1,0:T(8,128)(2,1)} %get-tuple-element.36.p_ref.grad_ref, bf16[32,576]{1,0:T(8,128)(2,1)} %get-tuple-element.37.edge_ref), custom_call_target="tpu_custom_call" | custom-call | tf_op jit(solution)/shard_map/pallas_call | solution.py:133
  74.7 17.1 %shard_map.168 = (bf16[192,2048]{1,0:T(8,128)(2,1)}, bf16[1024,128]{1,0:T(8,128)(2,1)}) custom-call(bf16[576,2048]{1,0:T(8,128)(2,1)} %get-tuple-element.36.p_ref.grad_ref, bf16[576,256]{1,0:T(8,128)(2,1)} %get-tuple-element.38.top_ref, bf16[576,256]{1,0:T(8,128)(2,1)} %get-tuple-element.39.bot_ref, bf16[2,3,16,576]{3,2,1,0:T(8,128)(2,1)} %get-tuple-element.40.side_ref, ...), custom_call_target="tpu_custom_call" | custom-call | tf_op jit(solution)/shard_map/pallas_call | solution.py:469
  91.8 2.2 %copy.22 = bf16[24,8,8,256]{3,2,1,0:T(8,128)(2,1)} copy(bf16[24,8,8,256]{3,1,2,0:T(8,128)(2,1)} %bitcast.27) | data formatting | bytes 1572864
  94.0 24.2 %shard_map.169.total_ref = bf16[1024,128]{1,0:T(8,128)(2,1)} custom-call(bf16[4,8,32,128]{3,2,1,0:T(8,128)(2,1)} %bitcast.28), custom_call_target="tpu_custom_call" | custom-call | tf_op jit(solution)/shard_map/pallas_call | solution.py:306
  118.2 1.8 %shard_map.170 = (f32[192,576]{1,0:T(8,128)}, f32[3,3,576]{2,1,0:T(4,128)}, f32[1,192]{1,0:T(1,128)}, f32[1,192]{1,0:T(1,128)}) custom-call(bf16[1024,128]{1,0:T(8,128)(2,1)} %shard_map.169.total_ref), custom_call_target="tpu_custom_call" | custom-call | tf_op jit(solution)/shard_map/pallas_call | solution.py:469
Async XLA Ops:
  0.6 3.9 %copy-start = (bf16[192,8,256]{2,1,0:T(8,128)(2,1)S(1)}, bf16[192,8,256]{2,1,0:T(8,128)(2,1)}, u32[]{:S(2)}) copy-start(bf16[192,8,256]{2,1,0:T(8,128)(2,1)} %param.12) | copy-start | bytes 2359300
